TPU v7x, 32 devices: a whole 2x2x4 slice. The times are simulated.
32 devices in a mesh: tok: 16 (over z, x, core), hid: 2 (over y).
Axes of the slice: x: 2, y: 2, z: 4, core: 2. Of those that a mesh axis runs over, the one named last changes fastest.
Arguments:
- base: float32 [512, 16384], P('tok', 'hid'), may hold values from -6 to 6
- source: float32 [512, 16384], P('tok', 'hid'), may hold values from -6 to 6
- pairs: int32 [512], replicated, may hold values from 0 to 511, each once
- counts: int32 [512], replicated, may hold values from 1 to 128
- rotation: float32 [16384, 16384], P('hid', 'tok'), may hold values from -0.046875 to 0.046875
Outputs:
- patched: float32 [512, 16384], P('tok', 'hid')
All inputs are finite; a program needn't handle non-finite values.
Results may differ from a plain program's by a relative error of at most 0.000075.
Values sent between devices are 32-bit elements; how exact they have to be, the bound alone decides.
A program may use at most 128 MiB of HBM per device.

v0:
```python
import jax
import jax.numpy as jnp
from jax import lax
from jax.sharding import PartitionSpec as P

BLOCK = 128


def local(base, source, pairs, counts, rotation):
    highest = lax.Precision.HIGHEST
    stacked = jnp.stack([base, source])
    terms = jnp.einsum(
        "srk,kc->src",
        lax.all_gather(stacked, "tok", axis=1, tiled=True),
        rotation,
        precision=highest,
        preferred_element_type=jnp.float32,
    )
    base_terms = terms[0]
    source_terms = jnp.take(terms[1], pairs, axis=0)
    width = rotation.shape[1]
    columns = lax.axis_index("tok") * width + jnp.arange(width, dtype=jnp.int32)
    summed = (
        lax.psum_scatter(base_terms, "hid", scatter_dimension=0, tiled=True),
        lax.psum_scatter(source_terms, "hid", scatter_dimension=0, tiled=True),
    )
    share = summed[0].shape[0]
    first = lax.axis_index("hid") * share
    limits = lax.dynamic_slice_in_dim(counts, first, share, 0) * BLOCK
    mixed = jnp.where(columns[None, :] < limits[:, None], summed[1], summed[0])
    full = lax.all_gather(mixed, "hid", axis=0, tiled=True)
    return lax.psum_scatter(
        lax.dot_general(
            full,
            rotation,
            (((1,), (1,)), ((), ())),
            precision=highest,
            preferred_element_type=jnp.float32,
        ),
        "tok",
        scatter_dimension=0,
        tiled=True,
    )


def solution(mesh):
    return jax.shard_map(
        local,
        mesh=mesh,
        in_specs=(P("tok", "hid"), P("tok", "hid"), P(), P(), P("hid", "tok")),
        out_specs=P("tok", "hid"),
        check_vma=False,
    )
```

profile of v0, /device:TPU:0, one launch (start us, length us, event | category | flops | bytes accessed | tf_op | source)
XLA Modules:
  0.0 646.5 jit_solution(1224443009447316070)
XLA Ops:
  6.5 0.0 all-gather.3.cloned.1.call-start
  6.5 3.0 pad_maximum_fusion
  9.6 0.0 copy-start
  9.6 0.0 all-gather.3.cloned.1.call-update
  9.6 0.0 reduce-scatter.4.cloned.1.call-start
  9.7 0.6 copy-done
  10.3 170.2 %all-gather.3.cloned.1.call-done = f32[2,512,8192]{2,1,0:T(8,128)} async-done(((f32[2,32,8192]{2,1,0:T(8,128)}), f32[2,512,8192]{2,1,0:T(8,128)}) %all-gather.3.cloned.1.call-update) | async-done | bytes 33554448 | tf_op jit(solution)/shard_map/all_gather | solution.py:14
  180.5 111.1 %fusion = f32[2,512,1024]{2,1,0:T(8,128)S(1)} fusion(f32[2,512,8192]{2,1,0:T(8,128)} %all-gather.3.cloned.1.call-done, f32[8192,1024]{1,0:T(8,128)} %param.9), kind=kOutput, calls=%fused_computation.1 | convolution fusion | flops 103079215104 | bytes 71303168 | tf_op jit(solution)/shard_map/srk,kc->src/dot_general | solution.py:12
  291.7 1.9 slice_bitcast_fusion
  293.5 2.7 gather_fusion
  296.2 3.1 broadcast_select_fusion
  299.3 0.0 copy-start.1
  299.3 0.0 reduce-scatter.4.cloned.1.call-update
  299.4 0.0 reduce-scatter.6.cloned.1.call-start
  299.4 0.7 reduce-scatter.6.cloned.1.call-update
  300.1 0.0 all-gather.5.cloned.1.call-start
  300.1 0.0 copy-done.1
  300.2 0.1 dynamic-slice_multiply_fusion
  300.2 31.1 %reduce-scatter.4.cloned.1.call-done = f32[256,1024]{1,0:T(8,128)} async-done(((f32[512,1024]{1,0:T(8,128)}), f32[256,1024]{1,0:T(8,128)}) %reduce-scatter.4.cloned.1.call-update) | async-done | bytes 1048592 | tf_op jit(solution)/shard_map/reduce_scatter | solution.py:25
  331.4 34.2 %reduce-scatter.6.cloned.1.call-done = f32[256,1024]{1,0:T(8,128)} async-done(((f32[512,1024]{1,0:T(8,128)}), f32[256,1024]{1,0:T(8,128)}) %reduce-scatter.6.cloned.1.call-update) | async-done | bytes 1048592 | tf_op jit(solution)/shard_map/reduce_scatter | solution.py:24
  365.6 2.7 compare_select_fusion
  368.2 0.0 all-gather.5.cloned.1.call-update
  368.3 0.0 reduce-scatter.8.cloned.1.call-start
  368.3 33.2 %all-gather.5.cloned.1.call-done = f32[512,1024]{1,0:T(8,128)} async-done(((f32[256,1024]{1,0:T(8,128)}), f32[512,1024]{1,0:T(8,128)}) %all-gather.5.cloned.1.call-update) | async-done | bytes 2097168 | tf_op jit(solution)/shard_map/all_gather | solution.py:31
  401.6 59.6 %fusion.2 = f32[512,8192]{1,0:T(8,128)} fusion(f32[512,1024]{1,0:T(8,128)} %all-gather.5.cloned.1.call-done, f32[8192,1024]{1,0:T(8,128)} %param.9), kind=kOutput, calls=%fused_computation.13 | convolution fusion | flops 51539607552 | bytes 52428800 | tf_op jit(solution)/shard_map/dot_general | solution.py:33
  461.2 0.0 reduce-scatter.8.cloned.1.call-update
  461.2 178.7 %reduce-scatter.8.cloned.1.call-done = f32[32,8192]{1,0:T(8,128)} async-done(((f32[512,8192]{1,0:T(8,128)}), f32[32,8192]{1,0:T(8,128)}) %reduce-scatter.8.cloned.1.call-update) | async-done | bytes 1048592 | tf_op jit(solution)/shard_map/reduce_scatter | solution.py:32
  (4 shorter events, 0.0 us)
Async XLA Ops:
  6.5 174.0 %all-gather.3.cloned.1.call-start = ((), (), s32[]{:S(2)}) async-start(), calls=%async_computation.3 | async-start | bytes 35651584 | tf_op jit(solution)/shard_map/all_gather | solution.py:14
  9.6 0.7 copy-start
  9.6 321.8 %reduce-scatter.4.cloned.1.call-start = ((), (), s32[]{:S(2)}) async-start(), calls=%async_computation.4 | async-start | bytes 3145728 | tf_op jit(solution)/shard_map/reduce_scatter | solution.py:25
  299.3 0.8 copy-start.1
  299.4 66.2 %reduce-scatter.6.cloned.1.call-start = ((), (), s32[]{:S(2)}) async-start(), calls=%async_computation.5 | async-start | bytes 3145728 | tf_op jit(solution)/shard_map/reduce_scatter | solution.py:24
  300.1 101.5 %all-gather.5.cloned.1.call-start = ((), (), s32[]{:S(2)}) async-start(), calls=%async_computation.6 | async-start | bytes 3145728 | tf_op jit(solution)/shard_map/all_gather | solution.py:31
  368.3 271.7 %reduce-scatter.8.cloned.1.call-start = ((), (), s32[]{:S(2)}) async-start(), calls=%async_computation.7 | async-start | bytes 17825792 | tf_op jit(solution)/shard_map/reduce_scatter | solution.py:32
Sparse Core Ops, SparseCore 0:
  9.7 170.7 all-gather.2
  299.5 31.8 reduce-scatter.3
  333.7 31.8 reduce-scatter.5
  368.4 33.1 all-gather.4
  461.3 178.5 reduce-scatter.7
where the time goes:
time: 647 us; the launch traced here: 646 us
  waiting for transfers between devices  448 us (69%)
  matrix products  171 us (26%)
  between operations  13.2 us (2%)
  other arithmetic  8.93 us (1%)
    reduce_scatter x1, waiting for transfers between devices, local(): lax.psum_scatter(lax.dot_general(full, rotation, (((1,), (1,)), ((), ()))...  179 us
    all_gather x1, waiting for transfers between devices, local(): lax.all_gather(stacked, 'tok', axis=1, tiled=True)  170 us
    dot_general x1, matrix products, local(): jnp.einsum('srk,kc->src', lax.all_gather(stacked, 'tok', axis=1, tiled=Tr...  111 us
    dot_general x1, matrix products, local(): lax.dot_general(full, rotation, (((1,), (1,)), ((), ())), precision=highe...  59.6 us
    reduce_scatter x1, waiting for transfers between devices, local(): lax.psum_scatter(base_terms, 'hid', scatter_dimension=0, tiled=True)  34.2 us
    all_gather x1, waiting for transfers between devices, local(): full = lax.all_gather(mixed, 'hid', axis=0, tiled=True)  33.2 us
    reduce_scatter x1, waiting for transfers between devices, local(): lax.psum_scatter(source_terms, 'hid', scatter_dimension=0, tiled=True)  31.1 us
  transfers between devices with their start and end apart: 5, of which 5 were waited for; matrix products, arithmetic and copies ran while one was open for 0% of the time, Pallas kernels for 0%

commit v1 on v0

v1 whole, which is shorter than its diff:
```python
import jax
import jax.numpy as jnp
from jax import lax
from jax.sharding import PartitionSpec as P

BLOCK = 128
K_PARTS = 4
ROW_PARTS = 4


def product(left, right, contract):
    return lax.dot_general(
        left,
        right,
        (contract, ((), ())),
        precision=lax.Precision.HIGH,
        preferred_element_type=jnp.float32,
    )


def local(tok, hid, base, source, pairs, counts, rotation):
    held, depth = base.shape
    width = rotation.shape[1]
    me = lax.axis_index("tok")
    core = lax.rem(me, 2)

    stacked = jnp.concatenate([base, source], axis=0)
    step = depth // K_PARTS
    terms = None
    for part in range(K_PARTS):
        rows = lax.all_gather(
            stacked[:, part * step : (part + 1) * step], "tok", axis=0, tiled=True
        )
        term = product(rows, rotation[part * step : (part + 1) * step], ((1,), (0,)))
        terms = term if terms is None else terms + term

    columns = me * width + jnp.arange(width, dtype=jnp.int32)
    share = held // ROW_PARTS
    chips = jnp.arange(tok // 2, dtype=jnp.int32)[:, None]
    within = jnp.arange(share, dtype=jnp.int32)[None, :]
    siblings = [(t, t ^ 1) for t in range(tok)]
    groups = [list(range(c, tok, 2)) for c in range(2)]

    def mix(part):
        index = jnp.concatenate(
            [
                ((chips * 2 + c) * held + part * share + within).reshape(-1)
                for c in (1 - core, core)
            ]
        )
        pair = pairs[index]
        base_at = (index // held) * (2 * held) + index % held
        source_at = (pair // held) * (2 * held) + held + pair % held
        limits = counts[index] * BLOCK
        return jnp.where(
            columns[None, :] < limits[:, None],
            terms.at[source_at].get(mode="promise_in_bounds"),
            terms.at[base_at].get(mode="promise_in_bounds"),
        )

    def summed_over_hid(mixed):
        if hid != 2:
            return lax.psum(mixed, "hid")
        return mixed + lax.ppermute(mixed, "hid", [(0, 1), (1, 0)])

    outs = []
    for part in range(ROW_PARTS):
        full = summed_over_hid(mix(part))
        partial = product(full, rotation, ((1,), (1,)))
        half = partial.shape[0] // 2
        mine = partial[half:] + lax.ppermute(partial[:half], "tok", siblings)
        outs.append(
            lax.psum_scatter(
                mine, "tok", scatter_dimension=0, axis_index_groups=groups, tiled=True
            )
        )
    return jnp.concatenate(outs, axis=0)


def solution(mesh):
    tok, hid = mesh.shape["tok"], mesh.shape["hid"]

    def run(*args):
        return local(tok, hid, *args)

    return jax.shard_map(
        run,
        mesh=mesh,
        in_specs=(P("tok", "hid"), P("tok", "hid"), P(), P(), P("hid", "tok")),
        out_specs=P("tok", "hid"),
        check_vma=False,
    )
```

time: 647 us -> 709 us (1.096)
  local copies, waits for them, and re-layouts: 5.16 us -> 52.9 us
  waiting for transfers between devices: 448 us -> 439 us
    reduce_scatter x3 -> x4, waiting for transfers between devices: 244 us -> 156 us  [local(): lax.psum_scatter(mine, 'tok', scatter_dimension=0, axis_index_groups=grou...]
    ppermute x0 -> x8, waiting for transfers between devices: none -> 50.1 us  [the longest x4 38.2 us: summed_over_hid(): return mixed + lax.ppermute(mixed, 'hid', [(0, 1), (1, 0)])]
    gather x1 -> x16, local copies, waits for them, and re-layouts: 2.67 us -> 40.7 us  [the longest x4 15.3 us: mix(): terms.at[source_at].get(mode='promise_in_bounds')]
    all_gather x2 -> x4, waiting for transfers between devices: 203 us -> 231 us  [local(): lax.all_gather(stacked[:, part * step:(part + 1) * step], 'tok', axis=0,...]
    slice x0 -> x5, local copies, waits for them, and re-layouts: none -> 8.94 us  [the longest x4 7.57 us: local(): mine = partial[half:] + lax.ppermute(partial[:half], 'tok', siblings)]
    dot_general x2 -> x8, matrix products: 171 us -> 177 us  [product(): lax.dot_general(left, right, (contract, ((), ())), precision=lax.Precisio...]
  transfers between devices with their start and end apart: 5 -> 16, of which waited for: 5 -> 15; matrix products, arithmetic and copies ran while one was open for 0% -> 22% of each run, Pallas kernels for 0% -> 0%
where the time goes in v1:
time: 709 us; the launch traced here: 702 us
  waiting for transfers between devices  439 us (62%)
  matrix products  177 us (25%)
  local copies, waits for them, and re-layouts  52.9 us (7%)
  between operations  14.4 us (2%)
  other arithmetic  11.8 us (2%)
    all_gather x4, waiting for transfers between devices, local(): lax.all_gather(stacked[:, part * step:(part + 1) * step], 'tok', axis=0,...  231 us
    dot_general x8, matrix products, product(): lax.dot_general(left, right, (contract, ((), ())), precision=lax.Precisio...  177 us
    reduce_scatter x4, waiting for transfers between devices, local(): lax.psum_scatter(mine, 'tok', scatter_dimension=0, axis_index_groups=grou...  156 us
    ppermute x4, waiting for transfers between devices, summed_over_hid(): return mixed + lax.ppermute(mixed, 'hid', [(0, 1), (1, 0)])  38.2 us
    gather x4, local copies, waits for them, and re-layouts, mix(): terms.at[source_at].get(mode='promise_in_bounds')  15.3 us
    gather x4, local copies, waits for them, and re-layouts, mix(): terms.at[base_at].get(mode='promise_in_bounds')  15.3 us
  transfers between devices with their start and end apart: 16, of which 15 were waited for; matrix products, arithmetic and copies ran while one was open for 22% of the time, Pallas kernels for 0%

profile of v1, /device:TPU:0, one launch (start us, length us, event | category | flops | bytes accessed | tf_op | source)
XLA Modules:
  0.0 701.9 jit_solution(6723186303921301951)
XLA Ops:
  6.5 1.3 constant_dynamic-update-slice_fusion.1
  7.9 1.3 constant_dynamic-update-slice_fusion
  9.2 1.4 fusion.38
  10.6 0.7 all-gather.9.cloned.1.call-update
  11.4 0.7 all-gather.7.cloned.1.call-update
  12.1 0.5 all-gather.5.cloned.1.call-update
  13.0 0.1 fusion.31
  13.1 1.3 gather_fusion.1
  14.4 1.3 gather_fusion
  15.8 0.1 concatenate.227
  16.0 0.1 fusion.33
  16.1 1.3 gather_fusion.5
  17.4 1.3 gather_fusion.4
  19.0 0.1 fusion.35
  19.1 1.3 gather_fusion.9
  20.4 1.3 gather_fusion.8
  21.9 0.1 fusion.37
  22.1 1.3 gather_fusion.13
  23.3 1.3 gather_fusion.12
  24.9 63.5 %all-gather.11.cloned.1.call-done = f32[1024,2048]{1,0:T(8,128)} async-done(((f32[64,2048]{1,0:T(8,128)}), f32[1024,2048]{1,0:T(8,128)}) %all-gather.11.cloned.1.call-update) | async-done | bytes 8388624 | tf_op jit(solution)/shard_map/all_gather | solution.py:31
  88.3 19.4 %fusion = f32[1024,1024]{1,0:T(8,128)} fusion(f32[1024,2048]{1,0:T(8,128)} %all-gather.11.cloned.1.call-done, f32[8192,1024]{1,0:T(8,128)} %param.9), kind=kOutput, calls=%fused_computation.16 | convolution fusion | flops 12884901888 | bytes 20971520 | tf_op jit(solution)/shard_map/dot_general | solution.py:12
  107.7 55.9 %all-gather.9.cloned.1.call-done = f32[1024,2048]{1,0:T(8,128)} async-done(((f32[64,2048]{1,0:T(8,128)}), f32[1024,2048]{1,0:T(8,128)}) %all-gather.9.cloned.1.call-update) | async-done | bytes 8388624 | tf_op jit(solution)/shard_map/all_gather | solution.py:31
  163.6 19.6 %fusion.2 = f32[1024,1024]{1,0:T(8,128)} fusion(f32[1024,2048]{1,0:T(8,128)} %all-gather.9.cloned.1.call-done, f32[8192,1024]{1,0:T(8,128)} %param.9), kind=kOutput, calls=%fused_computation.18 | convolution fusion | flops 12884901888 | bytes 20971520 | tf_op jit(solution)/shard_map/dot_general | solution.py:12
  183.3 55.7 %all-gather.7.cloned.1.call-done = f32[1024,2048]{1,0:T(8,128)} async-done(((f32[64,2048]{1,0:T(8,128)}), f32[1024,2048]{1,0:T(8,128)}) %all-gather.7.cloned.1.call-update) | async-done | bytes 8388624 | tf_op jit(solution)/shard_map/all_gather | solution.py:31
  239.0 19.4 %fusion.4 = f32[1024,1024]{1,0:T(8,128)} fusion(f32[1024,2048]{1,0:T(8,128)} %all-gather.7.cloned.1.call-done, f32[8192,1024]{1,0:T(8,128)} %param.9), kind=kOutput, calls=%fused_computation.20 | convolution fusion | flops 12884901888 | bytes 20971520 | tf_op jit(solution)/shard_map/dot_general | solution.py:12
  258.4 55.8 %all-gather.5.cloned.1.call-done = f32[1024,2048]{1,0:T(8,128)} async-done(((f32[64,2048]{1,0:T(8,128)}), f32[1024,2048]{1,0:T(8,128)}) %all-gather.5.cloned.1.call-update) | async-done | bytes 8388624 | tf_op jit(solution)/shard_map/all_gather | solution.py:31
  314.2 22.4 %add_add_fusion = f32[1024,1024]{1,0:T(8,128)} fusion(f32[1024,1024]{1,0:T(8,128)} %fusion, f32[1024,1024]{1,0:T(8,128)} %fusion.2, f32[1024,1024]{1,0:T(8,128)} %fusion.4, f32[1024,2048]{1,0:T(8,128)} %all-gather.5.cloned.1.call-done, f32[8192,1024]{1,0:T(8,128)} %param.9), kind=kOutput, calls=%fused_computation.24 | convolution fusion | flops 12888047616 | bytes 33554432 | tf_op jit(solution)/shard_map/dot_general | solution.py:12
  336.6 3.2 gather_fusion.2
  339.8 3.2 gather_fusion.3
  343.0 4.0 gather_fusion.6
  347.0 4.0 gather_fusion.7
  351.1 4.0 gather_fusion.10
  355.1 4.0 gather_fusion.11
  359.1 4.0 gather_fusion.14
  363.1 4.0 gather_fusion.15
  367.1 2.1 compare_select_fusion.3
  369.2 1.5 collective-permute-start.6
  370.8 12.6 %collective-permute-done.6 = f32[128,1024]{1,0:T(8,128)S(1)} collective-permute-done((f32[128,1024]{1,0:T(8,128)S(1)}, f32[128,1024]{1,0:T(8,128)S(1)}, u32[]{:S(2)}, u32[]{:S(2)}) %collective-permute-start.6) | collective-permute-done | bytes 524320 | tf_op jit(solution)/shard_map/ppermute | solution.py:64
  383.4 24.0 %fusion.10 = f32[128,8192]{1,0:T(8,128)} fusion(f32[8192,1024]{1,0:T(8,128)} %param.9, f32[128,1024]{1,0:T(8,128)S(1)} %get-tuple-element.12, f32[128,1024]{1,0:T(8,128)S(1)} %collective-permute-done.6), kind=kOutput, calls=%fused_computation.30 | convolution fusion | flops 6442582016 | bytes 38797312 | tf_op jit(solution)/shard_map/dot_general | solution.py:12
  407.4 1.9 slice.107
  409.3 1.6 collective-permute-start.4
  410.9 2.6 collective-permute-done.7
  413.5 1.6 slice_add_fusion
  415.2 8.5 %collective-permute-done.4 = f32[128,1024]{1,0:T(8,128)S(1)} collective-permute-done((f32[128,1024]{1,0:T(8,128)S(1)}, f32[128,1024]{1,0:T(8,128)S(1)}, u32[]{:S(2)}, u32[]{:S(2)}) %collective-permute-start.4) | collective-permute-done | bytes 524320 | tf_op jit(solution)/shard_map/ppermute | solution.py:64
  423.7 24.1 %fusion.12 = f32[128,8192]{1,0:T(8,128)} fusion(f32[8192,1024]{1,0:T(8,128)} %param.9, f32[128,1024]{1,0:T(8,128)S(1)} %get-tuple-element.11, f32[128,1024]{1,0:T(8,128)S(1)} %collective-permute-done.4), kind=kOutput, calls=%fused_computation.32 | convolution fusion | flops 6442582016 | bytes 38797312 | tf_op jit(solution)/shard_map/dot_general | solution.py:12
  447.8 1.9 slice.105
  449.8 1.6 collective-permute-start.2
  451.3 2.6 collective-permute-done.5
  453.9 1.6 slice_add_fusion.1
  455.6 8.5 %collective-permute-done.2 = f32[128,1024]{1,0:T(8,128)S(1)} collective-permute-done((f32[128,1024]{1,0:T(8,128)S(1)}, f32[128,1024]{1,0:T(8,128)S(1)}, u32[]{:S(2)}, u32[]{:S(2)}) %collective-permute-start.2) | collective-permute-done | bytes 524320 | tf_op jit(solution)/shard_map/ppermute | solution.py:64
  464.1 24.3 %fusion.14 = f32[128,8192]{1,0:T(8,128)} fusion(f32[8192,1024]{1,0:T(8,128)} %param.9, f32[128,1024]{1,0:T(8,128)S(1)} %get-tuple-element.10, f32[128,1024]{1,0:T(8,128)S(1)} %collective-permute-done.2), kind=kOutput, calls=%fused_computation.34 | convolution fusion | flops 6442582016 | bytes 38797312 | tf_op jit(solution)/shard_map/dot_general | solution.py:12
  488.4 1.9 slice.103
  490.3 1.6 collective-permute-start
  491.9 2.6 collective-permute-done.3
  494.5 1.6 slice_add_fusion.2
  496.2 8.5 %collective-permute-done = f32[128,1024]{1,0:T(8,128)S(1)} collective-permute-done((f32[128,1024]{1,0:T(8,128)S(1)}, f32[128,1024]{1,0:T(8,128)S(1)}, u32[]{:S(2)}, u32[]{:S(2)}) %collective-permute-start) | collective-permute-done | bytes 524320 | tf_op jit(solution)/shard_map/ppermute | solution.py:64
  504.7 24.2 %fusion.16 = f32[128,8192]{1,0:T(8,128)} fusion(f32[8192,1024]{1,0:T(8,128)} %param.9, f32[128,1024]{1,0:T(8,128)S(1)} %get-tuple-element.9, f32[128,1024]{1,0:T(8,128)S(1)} %collective-permute-done), kind=kOutput, calls=%fused_computation.36 | convolution fusion | flops 6442582016 | bytes 38797312 | tf_op jit(solution)/shard_map/dot_general | solution.py:12
  528.9 1.9 slice.101
  530.9 4.1 collective-permute-done.1
  535.1 1.6 slice_add_fusion.3
  536.7 14.8 %reduce-scatter.9.cloned.1.call-done = f32[8,8192]{1,0:T(8,128)} async-done(((f32[64,8192]{1,0:T(8,128)}), f32[8,8192]{1,0:T(8,128)}) %reduce-scatter.9.cloned.1.call-update) | async-done | bytes 262160 | tf_op jit(solution)/shard_map/reduce_scatter | solution.py:73
  551.5 70.4 %reduce-scatter.7.cloned.1.call-done = f32[8,8192]{1,0:T(8,128)} async-done(((f32[64,8192]{1,0:T(8,128)}), f32[8,8192]{1,0:T(8,128)}) %reduce-scatter.7.cloned.1.call-update) | async-done | bytes 262160 | tf_op jit(solution)/shard_map/reduce_scatter | solution.py:73
  621.9 70.4 %reduce-scatter.5.cloned.1.call-done = f32[8,8192]{1,0:T(8,128)} async-done(((f32[64,8192]{1,0:T(8,128)}), f32[8,8192]{1,0:T(8,128)}) %reduce-scatter.5.cloned.1.call-update) | async-done | bytes 262160 | tf_op jit(solution)/shard_map/reduce_scatter | solution.py:73
  692.3 2.2 pad_maximum_fusion
  (72 shorter events, 2.0 us)
Async XLA Ops:
  6.5 6.6 copy-start
  6.5 81.8 %all-gather.11.cloned.1.call-start = ((), (), s32[]{:S(2)}) async-start(), calls=%async_computation.7 | async-start | bytes 8912896 | tf_op jit(solution)/shard_map/all_gather | solution.py:31
  7.8 6.6 copy-start.2
  10.6 153.1 %all-gather.9.cloned.1.call-start = ((), (), s32[]{:S(2)}) async-start(), calls=%async_computation.6 | async-start | bytes 8912896 | tf_op jit(solution)/shard_map/all_gather | solution.py:31
  11.3 227.7 %all-gather.7.cloned.1.call-start = ((), (), s32[]{:S(2)}) async-start(), calls=%async_computation.5 | async-start | bytes 8912896 | tf_op jit(solution)/shard_map/all_gather | solution.py:31
  12.0 302.1 %all-gather.5.cloned.1.call-start = ((), (), s32[]{:S(2)}) async-start(), calls=%async_computation.4 | async-start | bytes 8912896 | tf_op jit(solution)/shard_map/all_gather | solution.py:31
  12.6 524.1 %reduce-scatter.11.cloned.1.call-start = ((), (), s32[]{:S(2)}) async-start(), calls=%async_computation.11 | async-start | bytes 2359296 | tf_op jit(solution)/shard_map/reduce_scatter | solution.py:73
  369.2 14.2 %collective-permute-start.6 = (f32[128,1024]{1,0:T(8,128)S(1)}, f32[128,1024]{1,0:T(8,128)S(1)}, u32[]{:S(2)}, u32[]{:S(2)}) collective-permute-start(f32[128,1024]{1,0:T(8,128)S(1)} %get-tuple-element.12), channel_id=1, source_target_pairs={{0,1},{1,0},{2,3},{3,2},{4,5},{5,4},{6,7},{7,6},{8,9},{9,8},{10,11... | collective-permute-start | bytes 1572872 | tf_op jit(solution)/shard_map/ppermute | solution.py:64
  407.4 6.1 copy-start.4
  409.3 4.2 collective-permute-start.7
  409.3 14.3 %collective-permute-start.4 = (f32[128,1024]{1,0:T(8,128)S(1)}, f32[128,1024]{1,0:T(8,128)S(1)}, u32[]{:S(2)}, u32[]{:S(2)}) collective-permute-start(f32[128,1024]{1,0:T(8,128)S(1)} %get-tuple-element.11), channel_id=1, source_target_pairs={{0,1},{1,0},{2,3},{3,2},{4,5},{5,4},{6,7},{7,6},{8,9},{9,8},{10,11... | collective-permute-start | bytes 1572872 | tf_op jit(solution)/shard_map/ppermute | solution.py:64
  415.1 136.4 %reduce-scatter.9.cloned.1.call-start = ((), (), s32[]{:S(2)}) async-start(), calls=%async_computation.10 | async-start | bytes 2359296 | tf_op jit(solution)/shard_map/reduce_scatter | solution.py:73
  447.8 6.1 copy-start.5
  449.7 4.2 collective-permute-start.5
  449.8 14.3 %collective-permute-start.2 = (f32[128,1024]{1,0:T(8,128)S(1)}, f32[128,1024]{1,0:T(8,128)S(1)}, u32[]{:S(2)}, u32[]{:S(2)}) collective-permute-start(f32[128,1024]{1,0:T(8,128)S(1)} %get-tuple-element.10), channel_id=1, source_target_pairs={{0,1},{1,0},{2,3},{3,2},{4,5},{5,4},{6,7},{7,6},{8,9},{9,8},{10,11... | collective-permute-start | bytes 1572872 | tf_op jit(solution)/shard_map/ppermute | solution.py:64
  455.5 166.4 %reduce-scatter.7.cloned.1.call-start = ((), (), s32[]{:S(2)}) async-start(), calls=%async_computation.9 | async-start | bytes 2359296 | tf_op jit(solution)/shard_map/reduce_scatter | solution.py:73
  488.4 6.1 copy-start.3
  490.3 4.2 collective-permute-start.3
  490.3 14.3 %collective-permute-start = (f32[128,1024]{1,0:T(8,128)S(1)}, f32[128,1024]{1,0:T(8,128)S(1)}, u32[]{:S(2)}, u32[]{:S(2)}) collective-permute-start(f32[128,1024]{1,0:T(8,128)S(1)} %get-tuple-element.9), channel_id=1, source_target_pairs={{0,1},{1,0},{2,3},{3,2},{4,5},{5,4},{6,7},{7,6},{8,9},{9,8},{10,11... | collective-permute-start | bytes 1572872 | tf_op jit(solution)/shard_map/ppermute | solution.py:64
  496.1 196.2 %reduce-scatter.5.cloned.1.call-start = ((), (), s32[]{:S(2)}) async-start(), calls=%async_computation.8 | async-start | bytes 2359296 | tf_op jit(solution)/shard_map/reduce_scatter | solution.py:73
  528.9 6.1 copy-start.6
  528.9 165.6 %copy-start.1 = (s32[512]{0:T(512)S(1)}, s32[512]{0:T(512)}, u32[]{:S(2)}) copy-start(s32[512]{0:T(512)} %param.7) | copy-start | bytes 6148
  530.9 4.2 collective-permute-start.1
Sparse Core Ops, SparseCore 0:
  10.7 77.5 all-gather.10
  90.5 73.1 all-gather.8
  165.8 73.1 all-gather.6
  241.0 73.1 all-gather.4
  415.2 65.9 reduce-scatter.10
  484.6 66.8 reduce-scatter.8
  555.0 66.8 reduce-scatter.6
  625.4 66.8 reduce-scatter.4

commit v2 on v1

v2 whole, which is shorter than its diff:
```python
import jax
import jax.numpy as jnp
from jax import lax
from jax.sharding import PartitionSpec as P

BLOCK = 128


def split(x):
    high = lax.reduce_precision(x, exponent_bits=8, mantissa_bits=7)
    return high.astype(jnp.bfloat16), (x - high).astype(jnp.bfloat16)


def product(left, right, contract):
    rows = left.shape[0]
    high, low = split(left)

    def dot(a, b):
        return lax.dot_general(
            a, b, (contract, ((), ())), preferred_element_type=jnp.float32
        )

    both = dot(jnp.concatenate([high, low], axis=0), right[0])
    return both[:rows] + (both[rows:] + dot(high, right[1]))


def local(tok, hid, base, source, pairs, counts, rotation):
    held, depth = base.shape
    width = rotation.shape[1]
    me = lax.axis_index("tok")
    core = lax.rem(me, 2)
    n = tok // 2

    order = list(range(0, n, 2)) + list(range(1, n, 2))[::-1]
    up = [
        (order[i] * 2 + c, order[(i + 1) % n] * 2 + c) for i in range(n) for c in (0, 1)
    ]
    down = [(b, a) for a, b in up]
    siblings = [(t, t ^ 1) for t in range(tok)]

    def place(chip):
        return jnp.where(chip % 2 == 0, chip // 2, n - 1 - chip // 2)

    def chip_at(position):
        return jnp.where(position * 2 < n, position * 2, (n - 1 - position) * 2 + 1)

    here = place(me // 2)

    weights = lax.optimization_barrier(split(rotation))

    terms, ready = [], []
    a, b = base, source
    for step in range(n):
        if step < n - 1:
            next_a = lax.ppermute(a, "tok", up)
            next_b = lax.ppermute(b, "tok", down)
        mine = jnp.concatenate([a, b], axis=0)
        other = lax.ppermute(mine, "tok", siblings)
        ready.append(jnp.concatenate([mine, other], axis=0))
        if step > 0:
            terms.append(product(ready[step - 1], weights, ((1,), (0,))))
        if step < n - 1:
            if step > 0:
                a, b, ready[step], terms[-1] = lax.optimization_barrier(
                    (next_a, next_b, ready[step], terms[-1])
                )
            else:
                a, b, ready[0], *weights = lax.optimization_barrier(
                    (next_a, next_b, ready[0], *weights)
                )
    terms.append(product(ready[n - 1], weights, ((1,), (0,))))
    terms = jnp.concatenate(terms, axis=0)

    def base_at(row):
        owner = row // held
        step = (here - place(owner // 2) + n) % n
        return step * 4 * held + (owner % 2 != core) * 2 * held + row % held

    def source_at(row):
        owner = row // held
        step = (place(owner // 2) - here + n) % n
        return step * 4 * held + (owner % 2 != core) * 2 * held + held + row % held

    columns = me * width + jnp.arange(width, dtype=jnp.int32)
    share = held // 2
    within = jnp.arange(share, dtype=jnp.int32)

    def rows_of(step):
        first = chip_at((here - 1 - step + 2 * n) % n)
        second = chip_at((here + 1 + step) % n)
        return [
            jnp.concatenate(
                [
                    (first * 2 + c) * held + within,
                    (second * 2 + c) * held + share + within,
                ]
            )
            for c in (core, 1 - core)
        ]

    def summed_over_hid(mixed):
        if hid != 2:
            return lax.psum(mixed, "hid")
        return mixed + lax.ppermute(mixed, "hid", [(0, 1), (1, 0)])

    group = 2
    parts = []
    for first in range(0, n, group):
        lists = [rows_of(first + i) for i in range(group)]
        index = jnp.concatenate([l[0] for l in lists] + [l[1] for l in lists])
        limits = counts[index] * BLOCK
        mixed = jnp.where(
            columns[None, :] < limits[:, None],
            terms.at[source_at(pairs[index])].get(mode="promise_in_bounds"),
            terms.at[base_at(index)].get(mode="promise_in_bounds"),
        )
        parts.append(summed_over_hid(mixed))

    def summed_over_cores(partial):
        half = partial.shape[0] // 2
        return partial[:half] + lax.ppermute(partial[half:], "tok", siblings)

    a = b = None
    mine = summed_over_cores(product(parts[0], weights, ((1,), (1,))))
    for number in range(len(parts)):
        later = None
        if number + 1 < len(parts):
            mine, full = lax.optimization_barrier((mine, parts[number + 1]))
            later = product(full, weights, ((1,), (1,)))
        for i in range(group):
            here_a = mine[2 * i * share : (2 * i + 1) * share]
            here_b = mine[(2 * i + 1) * share : (2 * i + 2) * share]
            a = here_a if a is None else here_a + a
            b = here_b if b is None else here_b + b
            if number * group + i < n - 1:
                a = lax.ppermute(a, "tok", up)
                b = lax.ppermute(b, "tok", down)
                if i == 0 and later is not None:
                    a, b, later = lax.optimization_barrier((a, b, later))
                else:
                    a, b = lax.optimization_barrier((a, b))
        if later is not None:
            mine = summed_over_cores(later)
    return jnp.concatenate([a, b], axis=0)


def solution(mesh):
    tok, hid = mesh.shape["tok"], mesh.shape["hid"]

    def run(*args):
        return local(tok, hid, *args)

    return jax.shard_map(
        run,
        mesh=mesh,
        in_specs=(P("tok", "hid"), P("tok", "hid"), P(), P(), P("hid", "tok")),
        out_specs=P("tok", "hid"),
        check_vma=False,
    )
```

time: 709 us -> 501 us (0.71)
  waiting for transfers between devices: 439 us -> 87.6 us
  other arithmetic: 11.8 us -> 83.9 us
  matrix products: 177 us -> 234 us
  starting transfers between devices: 6.75 us -> 36.7 us
  between operations: 14.4 us -> 1.4 us
    all_gather x4 -> x0, waiting for transfers between devices: 231 us -> none  [local(): lax.all_gather(stacked[:, part * step:(part + 1) * step], 'tok', axis=0,...]
    reduce_scatter x4 -> x0, waiting for transfers between devices: 156 us -> none  [local(): lax.psum_scatter(mine, 'tok', scatter_dimension=0, axis_index_groups=grou...]
    dot_general x8 -> x24, matrix products: 177 us -> 234 us  [dot(): lax.dot_general(a, b, (contract, ((), ())), preferred_element_type=jnp.fl...]
    ppermute x4 -> x40, waiting for transfers between devices: 11.9 us -> 62.1 us  [the longest x7 44.4 us: local(): a = lax.ppermute(a, 'tok', up)]
    convert_element_type x0 -> x13, other arithmetic: none -> 33.6 us  [split(): return (high.astype(jnp.bfloat16), (x - high).astype(jnp.bfloat16))]
    ppermute x4 -> x40, starting transfers between devices: 0.28 us -> 31.5 us  [the longest x7 13.1 us: local(): next_a = lax.ppermute(a, 'tok', up)]
    concatenate x1 -> x48, other arithmetic: 2.22 us -> 33 us  [the longest x7 16.1 us: local(): ready.append(jnp.concatenate([mine, other], axis=0))]
    ppermute x4, waiting for transfers between devices: 38.2 us -> 25.5 us  [summed_over_hid(): return mixed + lax.ppermute(mixed, 'hid', [(0, 1), (1, 0)])]
  transfers between devices with their start and end apart: 16 -> 44, of which waited for: 15 -> 20; matrix products, arithmetic and copies ran while one was open for 22% -> 57% of each run, Pallas kernels for 0% -> 0%
where the time goes in v2:
time: 501 us; the launch traced here: 496 us
  matrix products  234 us (47%)
  waiting for transfers between devices  87.6 us (17%)
  other arithmetic  83.9 us (17%)
  local copies, waits for them, and re-layouts  52.2 us (10%)
  starting transfers between devices  36.7 us (7%)
    dot_general x24, matrix products, dot(): lax.dot_general(a, b, (contract, ((), ())), preferred_element_type=jnp.fl...  234 us
    ppermute x7, waiting for transfers between devices, local(): a = lax.ppermute(a, 'tok', up)  44.4 us
    convert_element_type x13, other arithmetic, split(): return (high.astype(jnp.bfloat16), (x - high).astype(jnp.bfloat16))  33.6 us
    ppermute x4, waiting for transfers between devices, summed_over_hid(): return mixed + lax.ppermute(mixed, 'hid', [(0, 1), (1, 0)])  25.5 us
    concatenate x7, other arithmetic, local(): ready.append(jnp.concatenate([mine, other], axis=0))  16.1 us
    gather x4, local copies, waits for them, and re-layouts, local(): terms.at[base_at(index)].get(mode='promise_in_bounds')  15.8 us
    concatenate x8, other arithmetic, local(): mine = jnp.concatenate([a, b], axis=0)  15.7 us
    gather x4, local copies, waits for them, and re-layouts, local(): terms.at[source_at(pairs[index])].get(mode='promise_in_bounds')  15 us
  transfers between devices with their start and end apart: 44, of which 20 were waited for; matrix products, arithmetic and copies ran while one was open for 57% of the time, Pallas kernels for 0%

profile of v2, /device:TPU:0, one launch (start us, length us, event | category | flops | bytes accessed | tf_op | source)
XLA Modules:
  0.0 495.6 jit_solution(1803851837660200541)
XLA Ops:
  0.0 3.0 collective-permute-start
  3.0 3.0 pad_maximum_fusion.7
  22.4 19.1 %fusion = (bf16[8192,1024]{1,0:T(8,128)(2,1)S(1)}, bf16[8192,1024]{1,0:T(8,128)(2,1)}) fusion(f32[8192,1024]{1,0:T(8,128)} %param.9), kind=kLoop, calls=%fused_computation.18 | loop fusion | flops 33554432 | bytes 67108864 | tf_op jit(solution)/shard_map/convert_element_type | solution.py:11
  42.1 3.6 pad_maximum_fusion
  45.8 2.1 collective-permute-start.3
  50.0 1.8 fusion.1
  51.8 12.0 %fusion.13 = f32[256,1024]{1,0:T(8,128)} fusion(bf16[8192,1024]{1,0:T(8,128)(2,1)} %get-tuple-element.64, bf16[128,8192]{1,0:T(8,128)(2,1)} %get-tuple-element.129, bf16[128,8192]{1,0:T(8,128)(2,1)S(1)} %get-tuple-element.130), kind=kOutput, calls=%fused_computation.53 | convolution fusion | flops 4303355904 | bytes 22020096 | tf_op jit(solution)/shard_map/dot_general | solution.py:19
  63.8 3.7 fusion.58
  67.5 2.1 pad_maximum_fusion.1
  69.7 1.9 collective-permute-done.3
  71.6 2.0 collective-permute-done.4
  77.3 1.8 fusion.2
  79.1 12.0 %fusion.17 = f32[256,1024]{1,0:T(8,128)} fusion(bf16[8192,1024]{1,0:T(8,128)(2,1)} %get-tuple-element.64, bf16[128,8192]{1,0:T(8,128)(2,1)} %get-tuple-element.127, bf16[128,8192]{1,0:T(8,128)(2,1)S(1)} %get-tuple-element.128), kind=kOutput, calls=%fused_computation.58 | convolution fusion | flops 4303355904 | bytes 22020096 | tf_op jit(solution)/shard_map/dot_general | solution.py:19
  91.1 4.5 fusion.57
  96.4 2.0 pad_maximum_fusion.2
  103.2 1.8 fusion.3
  105.0 12.0 %fusion.21 = f32[256,1024]{1,0:T(8,128)} fusion(bf16[8192,1024]{1,0:T(8,128)(2,1)} %get-tuple-element.64, bf16[128,8192]{1,0:T(8,128)(2,1)} %get-tuple-element.125, bf16[128,8192]{1,0:T(8,128)(2,1)S(1)} %get-tuple-element.126), kind=kOutput, calls=%fused_computation.63 | convolution fusion | flops 4303355904 | bytes 22020096 | tf_op jit(solution)/shard_map/dot_general | solution.py:19
  117.0 3.7 fusion.56
  121.6 2.0 pad_maximum_fusion.3
  129.4 1.8 fusion.4
  131.3 12.0 %fusion.25 = f32[256,1024]{1,0:T(8,128)} fusion(bf16[8192,1024]{1,0:T(8,128)(2,1)} %get-tuple-element.64, bf16[128,8192]{1,0:T(8,128)(2,1)} %get-tuple-element.123, bf16[128,8192]{1,0:T(8,128)(2,1)S(1)} %get-tuple-element.124), kind=kOutput, calls=%fused_computation.68 | convolution fusion | flops 4303355904 | bytes 22020096 | tf_op jit(solution)/shard_map/dot_general | solution.py:19
  143.3 3.7 fusion.55
  147.8 2.0 pad_maximum_fusion.4
  155.0 1.8 fusion.5
  156.8 8.9 %fusion.29 = f32[256,1024]{1,0:T(8,128)S(1)} fusion(bf16[8192,1024]{1,0:T(8,128)(2,1)} %get-tuple-element.64, bf16[128,8192]{1,0:T(8,128)(2,1)} %get-tuple-element.121, bf16[128,8192]{1,0:T(8,128)(2,1)S(1)} %get-tuple-element.122), kind=kOutput, calls=%fused_computation.73 | convolution fusion | flops 4303355904 | bytes 22020096 | tf_op jit(solution)/shard_map/dot_general | solution.py:19
  165.7 3.3 fusion.54
  169.8 2.0 pad_maximum_fusion.5
  171.8 3.6 collective-permute-done.15
  179.0 2.8 pad_maximum_fusion.13
  182.5 9.2 %fusion.33 = f32[256,1024]{1,0:T(8,128)} fusion(bf16[8192,1024]{1,0:T(8,128)(2,1)} %get-tuple-element.64, bf16[128,8192]{1,0:T(8,128)(2,1)S(1)} %get-tuple-element.119, bf16[128,8192]{1,0:T(8,128)(2,1)S(1)} %get-tuple-element.120), kind=kOutput, calls=%fused_computation.78 | convolution fusion | flops 4303355904 | bytes 22020096 | tf_op jit(solution)/shard_map/dot_general | solution.py:19
  191.7 4.5 fusion.53
  197.1 2.3 pad_maximum_fusion.6
  199.5 2.6 collective-permute-done.19
  202.1 1.8 fusion.7
  205.2 2.7 pad_maximum_fusion.14
  207.9 12.0 %fusion.37 = f32[256,1024]{1,0:T(8,128)} fusion(bf16[8192,1024]{1,0:T(8,128)(2,1)} %get-tuple-element.64, bf16[128,8192]{1,0:T(8,128)(2,1)} %get-tuple-element.117, bf16[128,8192]{1,0:T(8,128)(2,1)S(1)} %get-tuple-element.118), kind=kOutput, calls=%fused_computation.82 | convolution fusion | flops 4303355904 | bytes 22020096 | tf_op jit(solution)/shard_map/dot_general | solution.py:19
  219.9 1.9 constant_dynamic-update-slice_fusion.3
  221.9 4.5 fusion.52
  228.1 1.8 fusion.8
  229.9 9.1 %fusion.41 = f32[256,1024]{1,0:T(8,128)S(1)} fusion(bf16[8192,1024]{1,0:T(8,128)(2,1)} %get-tuple-element.64, bf16[128,8192]{1,0:T(8,128)(2,1)} %get-tuple-element.115, bf16[128,8192]{1,0:T(8,128)(2,1)S(1)} %get-tuple-element.116), kind=kOutput, calls=%fused_computation.86 | convolution fusion | flops 4303355904 | bytes 22020096 | tf_op jit(solution)/shard_map/dot_general | solution.py:19
  239.0 3.3 fusion.50
  242.3 3.4 gather_fusion.14
  245.6 3.4 gather_fusion.15
  249.0 3.4 gather_fusion.6
  252.4 4.1 gather_fusion.7
  256.5 4.1 gather_fusion.10
  260.6 4.1 gather_fusion.11
  264.8 4.1 gather_fusion.2
  268.9 4.1 gather_fusion.3
  273.1 2.0 compare_select_fusion
  276.7 12.8 %collective-permute-done.22 = f32[128,1024]{1,0:T(8,128)S(1)} collective-permute-done((f32[128,1024]{1,0:T(8,128)S(1)}, f32[128,1024]{1,0:T(8,128)S(1)}, u32[]{:S(2)}, u32[]{:S(2)}) %collective-permute-start.22) | collective-permute-done | bytes 524320 | tf_op jit(solution)/shard_map/ppermute | solution.py:104
  289.6 19.3 %fusion.59 = f32[256,8192]{1,0:T(8,128)} fusion(bf16[8192,1024]{1,0:T(8,128)(2,1)} %get-tuple-element.64, bf16[128,1024]{1,0:T(8,128)(2,1)S(1)} %get-tuple-element.147, bf16[128,1024]{1,0:T(8,128)(2,1)S(1)} %get-tuple-element.148), kind=kOutput, calls=%fused_computation.137 | convolution fusion | flops 4296015872 | bytes 25690112 | tf_op jit(solution)/shard_map/dot_general | solution.py:19
  308.9 11.1 %fusion.12 = f32[128,8192]{1,0:T(8,128)S(1)} fusion(f32[256,8192]{1,0:T(8,128)} %fusion.59, bf16[128,1024]{1,0:T(8,128)(2,1)S(1)} %get-tuple-element.148, bf16[8192,1024]{1,0:T(8,128)(2,1)} %copy-done.2), kind=kOutput, calls=%fused_computation.50 | convolution fusion | flops 2149580800 | bytes 29622272 | tf_op jit(solution)/shard_map/dot_general | solution.py:19
  322.3 12.7 %collective-permute-done.24 = f32[128,1024]{1,0:T(8,128)S(1)} collective-permute-done((f32[128,1024]{1,0:T(8,128)S(1)}, f32[128,1024]{1,0:T(8,128)S(1)}, u32[]{:S(2)}, u32[]{:S(2)}) %collective-permute-start.24) | collective-permute-done | bytes 524320 | tf_op jit(solution)/shard_map/ppermute | solution.py:104
  339.2 13.7 %fusion.63 = f32[256,8192]{1,0:T(8,128)} fusion(bf16[8192,1024]{1,0:T(8,128)(2,1)} %get-tuple-element.64, bf16[128,1024]{1,0:T(8,128)(2,1)} %get-tuple-element.153, bf16[128,1024]{1,0:T(8,128)(2,1)S(1)} %get-tuple-element.154), kind=kOutput, calls=%fused_computation.141 | convolution fusion | flops 4296015872 | bytes 25690112 | tf_op jit(solution)/shard_map/dot_general | solution.py:19
  352.9 11.3 %fusion.11 = f32[128,8192]{1,0:T(8,128)S(1)} fusion(f32[256,8192]{1,0:T(8,128)} %fusion.63, bf16[128,1024]{1,0:T(8,128)(2,1)S(1)} %get-tuple-element.154, bf16[8192,1024]{1,0:T(8,128)(2,1)} %copy-done.2), kind=kOutput, calls=%fused_computation.48 | convolution fusion | flops 2149580800 | bytes 29622272 | tf_op jit(solution)/shard_map/dot_general | solution.py:19
  370.6 9.6 %collective-permute-done.29 = f32[16,8192]{1,0:T(8,128)S(1)} collective-permute-done((f32[16,8192]{1,0:T(8,128)S(1)}, f32[16,8192]{1,0:T(8,128)S(1)}, u32[]{:S(2)}, u32[]{:S(2)}) %collective-permute-start.29) | collective-permute-done | bytes 524320 | tf_op jit(solution)/shard_map/ppermute | solution.py:136
  384.3 18.9 %fusion.67 = f32[256,8192]{1,0:T(8,128)} fusion(bf16[8192,1024]{1,0:T(8,128)(2,1)} %get-tuple-element.64, bf16[128,1024]{1,0:T(8,128)(2,1)S(1)} %get-tuple-element.151, bf16[128,1024]{1,0:T(8,128)(2,1)S(1)} %get-tuple-element.152), kind=kOutput, calls=%fused_computation.145 | convolution fusion | flops 4296015872 | bytes 25690112 | tf_op jit(solution)/shard_map/dot_general | solution.py:19
  403.2 11.1 %fusion.10 = f32[128,8192]{1,0:T(8,128)S(1)} fusion(f32[256,8192]{1,0:T(8,128)} %fusion.67, bf16[128,1024]{1,0:T(8,128)(2,1)S(1)} %get-tuple-element.152, bf16[8192,1024]{1,0:T(8,128)(2,1)} %copy-done.2), kind=kOutput, calls=%fused_computation.46 | convolution fusion | flops 2149580800 | bytes 29622272 | tf_op jit(solution)/shard_map/dot_general | solution.py:19
  419.1 11.1 %collective-permute-done.35 = f32[16,8192]{1,0:T(8,128)S(1)} collective-permute-done((f32[16,8192]{1,0:T(8,128)S(1)}, f32[16,8192]{1,0:T(8,128)S(1)}, u32[]{:S(2)}, u32[]{:S(2)}) %collective-permute-start.35) | collective-permute-done | bytes 524320 | tf_op jit(solution)/shard_map/ppermute | solution.py:136
  434.1 19.1 %fusion.71 = f32[256,8192]{1,0:T(8,128)} fusion(bf16[8192,1024]{1,0:T(8,128)(2,1)} %get-tuple-element.64, bf16[128,1024]{1,0:T(8,128)(2,1)S(1)} %get-tuple-element.149, bf16[128,1024]{1,0:T(8,128)(2,1)S(1)} %get-tuple-element.150), kind=kOutput, calls=%fused_computation.149 | convolution fusion | flops 4296015872 | bytes 25690112 | tf_op jit(solution)/shard_map/dot_general | solution.py:19
  453.2 11.1 %fusion.9 = f32[128,8192]{1,0:T(8,128)S(1)} fusion(f32[256,8192]{1,0:T(8,128)} %fusion.71, bf16[128,1024]{1,0:T(8,128)(2,1)S(1)} %get-tuple-element.150, bf16[8192,1024]{1,0:T(8,128)(2,1)} %copy-done.2), kind=kOutput, calls=%fused_computation.44 | convolution fusion | flops 2149580800 | bytes 29622272 | tf_op jit(solution)/shard_map/dot_general | solution.py:19
  467.8 12.3 %collective-permute-done.40 = f32[16,8192]{1,0:T(8,128)S(1)} collective-permute-done((f32[16,8192]{1,0:T(8,128)S(1)}, f32[16,8192]{1,0:T(8,128)S(1)}, u32[]{:S(2)}, u32[]{:S(2)}) %collective-permute-start.40) | collective-permute-done | bytes 524320 | tf_op jit(solution)/shard_map/ppermute | solution.py:136
  482.7 11.3 %collective-permute-done.42 = f32[16,8192]{1,0:T(8,128)S(1)} collective-permute-done((f32[16,8192]{1,0:T(8,128)S(1)}, f32[16,8192]{1,0:T(8,128)S(1)}, u32[]{:S(2)}, u32[]{:S(2)}) %collective-permute-start.42) | collective-permute-done | bytes 524320 | tf_op jit(solution)/shard_map/ppermute | solution.py:136
  (205 shorter events, 84.2 us)
Async XLA Ops:
  0.0 6.6 %copy-start = (s32[512]{0:T(512)S(1)}, s32[512]{0:T(512)}, u32[]{:S(2)}) copy-start(s32[512]{0:T(512)} %param.7) | copy-start | bytes 6148
  0.0 9.1 %copy-start.3 = (s32[512]{0:T(512)S(1)}, s32[512]{0:T(512)}, u32[]{:S(2)}) copy-start(s32[512]{0:T(512)} %param.8) | copy-start | bytes 6148
  0.0 45.8 %collective-permute-start = (f32[32,8192]{1,0:T(8,128)}, f32[32,8192]{1,0:T(8,128)S(1)}, u32[]{:S(2)}, u32[]{:S(2)}) collective-permute-start(f32[32,8192]{1,0:T(8,128)} %param.5), channel_id=1, source_target_pairs={{0,8},{2,10},{8,16},{10,18},{16,24},{18,26},{24,28},{26,30},{28,20... | collective-permute-start | bytes 3145736 | tf_op jit(solution)/shard_map/ppermute | solution.py:55
  3.0 42.7 %collective-permute-start.1 = (f32[32,8192]{1,0:T(8,128)}, f32[32,8192]{1,0:T(8,128)S(1)}, u32[]{:S(2)}, u32[]{:S(2)}) collective-permute-start(f32[32,8192]{1,0:T(8,128)} %param.6), channel_id=1, source_target_pairs={{8,0},{10,2},{16,8},{18,10},{24,16},{26,18},{28,24},{30,26},{20,28... | collective-permute-start | bytes 3145736 | tf_op jit(solution)/shard_map/ppermute | solution.py:56
  6.0 36.1 %collective-permute-start.2 = (f32[64,8192]{1,0:T(8,128)}, f32[64,8192]{1,0:T(8,128)}, u32[]{:S(2)}, u32[]{:S(2)}) collective-permute-start(f32[64,8192]{1,0:T(8,128)} %pad_maximum_fusion.7), channel_id=1, source_target_pairs={{0,2},{2,0},{4,6},{6,4},{8,10},{10,8},{12,14},{14,12},{16,18},{18,... | collective-permute-start | bytes 6291464 | tf_op jit(solution)/shard_map/ppermute | solution.py:58
  22.4 19.8 %copy-start.5 = (f32[32,8192]{1,0:T(8,128)S(1)}, f32[32,8192]{1,0:T(8,128)}, u32[]{:S(2)}) copy-start(f32[32,8192]{1,0:T(8,128)} %param.5) | copy-start | bytes 3145732
  22.4 19.8 %copy-start.6 = (f32[32,8192]{1,0:T(8,128)S(1)}, f32[32,8192]{1,0:T(8,128)}, u32[]{:S(2)}) copy-start(f32[32,8192]{1,0:T(8,128)} %param.6) | copy-start | bytes 3145732
  41.5 197.5 %copy-start.2 = (bf16[8192,1024]{1,0:T(8,128)(2,1)}, bf16[8192,1024]{1,0:T(8,128)(2,1)S(1)}, u32[]{:S(2)}) copy-start(bf16[8192,1024]{1,0:T(8,128)(2,1)S(1)} %get-tuple-element.65) | copy-start | bytes 50331652
  45.8 25.8 %collective-permute-start.3 = (f32[32,8192]{1,0:T(8,128)S(1)}, f32[32,8192]{1,0:T(8,128)S(1)}, u32[]{:S(2)}, u32[]{:S(2)}) collective-permute-start(f32[32,8192]{1,0:T(8,128)S(1)} %collective-permute-done), channel_id=1, source_target_pairs={{0,8},{2,10},{8,16},{10,18},{16,24},{18,26},{24,28},{26,30},{28,20... | collective-permute-start | bytes 3145736 | tf_op jit(solution)/shard_map/ppermute | solution.py:55
  47.9 25.8 %collective-permute-start.4 = (f32[32,8192]{1,0:T(8,128)S(1)}, f32[32,8192]{1,0:T(8,128)S(1)}, u32[]{:S(2)}, u32[]{:S(2)}) collective-permute-start(f32[32,8192]{1,0:T(8,128)S(1)} %collective-permute-done.1), channel_id=1, source_target_pairs={{8,0},{10,2},{16,8},{18,10},{24,16},{26,18},{28,24},{30,26},{20,28... | collective-permute-start | bytes 3145736 | tf_op jit(solution)/shard_map/ppermute | solution.py:56
  49.8 17.7 %collective-permute-start.5 = (f32[64,8192]{1,0:T(8,128)}, f32[64,8192]{1,0:T(8,128)}, u32[]{:S(2)}, u32[]{:S(2)}) collective-permute-start(f32[64,8192]{1,0:T(8,128)} %pad_maximum_fusion.8), channel_id=1, source_target_pairs={{0,2},{2,0},{4,6},{6,4},{8,10},{10,8},{12,14},{14,12},{16,18},{18,... | collective-permute-start | bytes 6291464 | tf_op jit(solution)/shard_map/ppermute | solution.py:58
  73.6 24.8 %collective-permute-start.6 = (f32[32,8192]{1,0:T(8,128)S(1)}, f32[32,8192]{1,0:T(8,128)S(1)}, u32[]{:S(2)}, u32[]{:S(2)}) collective-permute-start(f32[32,8192]{1,0:T(8,128)S(1)} %collective-permute-done.3), channel_id=1, source_target_pairs={{0,8},{2,10},{8,16},{10,18},{16,24},{18,26},{24,28},{26,30},{28,20... | collective-permute-start | bytes 3145736 | tf_op jit(solution)/shard_map/ppermute | solution.py:55
  75.2 24.3 %collective-permute-start.7 = (f32[32,8192]{1,0:T(8,128)S(1)}, f32[32,8192]{1,0:T(8,128)S(1)}, u32[]{:S(2)}, u32[]{:S(2)}) collective-permute-start(f32[32,8192]{1,0:T(8,128)S(1)} %collective-permute-done.4), channel_id=1, source_target_pairs={{8,0},{10,2},{16,8},{18,10},{24,16},{26,18},{28,24},{30,26},{20,28... | collective-permute-start | bytes 3145736 | tf_op jit(solution)/shard_map/ppermute | solution.py:56
  77.3 19.2 %collective-permute-start.8 = (f32[64,8192]{1,0:T(8,128)}, f32[64,8192]{1,0:T(8,128)}, u32[]{:S(2)}, u32[]{:S(2)}) collective-permute-start(f32[64,8192]{1,0:T(8,128)} %pad_maximum_fusion.9), channel_id=1, source_target_pairs={{0,2},{2,0},{4,6},{6,4},{8,10},{10,8},{12,14},{14,12},{16,18},{18,... | collective-permute-start | bytes 6291464 | tf_op jit(solution)/shard_map/ppermute | solution.py:58
  99.5 24.6 %collective-permute-start.9 = (f32[32,8192]{1,0:T(8,128)S(1)}, f32[32,8192]{1,0:T(8,128)S(1)}, u32[]{:S(2)}, u32[]{:S(2)}) collective-permute-start(f32[32,8192]{1,0:T(8,128)S(1)} %collective-permute-done.6), channel_id=1, source_target_pairs={{0,8},{2,10},{8,16},{10,18},{16,24},{18,26},{24,28},{26,30},{28,20... | collective-permute-start | bytes 3145736 | tf_op jit(solution)/shard_map/ppermute | solution.py:55
  101.1 24.5 %collective-permute-start.10 = (f32[32,8192]{1,0:T(8,128)S(1)}, f32[32,8192]{1,0:T(8,128)S(1)}, u32[]{:S(2)}, u32[]{:S(2)}) collective-permute-start(f32[32,8192]{1,0:T(8,128)S(1)} %collective-permute-done.7), channel_id=1, source_target_pairs={{8,0},{10,2},{16,8},{18,10},{24,16},{26,18},{28,24},{30,26},{20,28... | collective-permute-start | bytes 3145736 | tf_op jit(solution)/shard_map/ppermute | solution.py:56
  103.2 18.4 %collective-permute-start.11 = (f32[64,8192]{1,0:T(8,128)}, f32[64,8192]{1,0:T(8,128)}, u32[]{:S(2)}, u32[]{:S(2)}) collective-permute-start(f32[64,8192]{1,0:T(8,128)} %pad_maximum_fusion.10), channel_id=1, source_target_pairs={{0,2},{2,0},{4,6},{6,4},{8,10},{10,8},{12,14},{14,12},{16,18},{18,... | collective-permute-start | bytes 6291464 | tf_op jit(solution)/shard_map/ppermute | solution.py:58
  117.0 3.8 copy-start.8
  125.6 24.3 %collective-permute-start.12 = (f32[32,8192]{1,0:T(8,128)S(1)}, f32[32,8192]{1,0:T(8,128)S(1)}, u32[]{:S(2)}, u32[]{:S(2)}) collective-permute-start(f32[32,8192]{1,0:T(8,128)S(1)} %collective-permute-done.9), channel_id=1, source_target_pairs={{0,8},{2,10},{8,16},{10,18},{16,24},{18,26},{24,28},{26,30},{28,20... | collective-permute-start | bytes 3145736 | tf_op jit(solution)/shard_map/ppermute | solution.py:55
  127.2 24.3 %collective-permute-start.13 = (f32[32,8192]{1,0:T(8,128)S(1)}, f32[32,8192]{1,0:T(8,128)S(1)}, u32[]{:S(2)}, u32[]{:S(2)}) collective-permute-start(f32[32,8192]{1,0:T(8,128)S(1)} %collective-permute-done.10), channel_id=1, source_target_pairs={{8,0},{10,2},{16,8},{18,10},{24,16},{26,18},{28,24},{30,26},{20,28... | collective-permute-start | bytes 3145736 | tf_op jit(solution)/shard_map/ppermute | solution.py:56
  129.4 18.4 %collective-permute-start.14 = (f32[64,8192]{1,0:T(8,128)}, f32[64,8192]{1,0:T(8,128)}, u32[]{:S(2)}, u32[]{:S(2)}) collective-permute-start(f32[64,8192]{1,0:T(8,128)} %pad_maximum_fusion.11), channel_id=1, source_target_pairs={{0,2},{2,0},{4,6},{6,4},{8,10},{10,8},{12,14},{14,12},{16,18},{18,... | collective-permute-start | bytes 6291464 | tf_op jit(solution)/shard_map/ppermute | solution.py:58
  151.5 24.0 %collective-permute-start.15 = (f32[32,8192]{1,0:T(8,128)S(1)}, f32[32,8192]{1,0:T(8,128)S(1)}, u32[]{:S(2)}, u32[]{:S(2)}) collective-permute-start(f32[32,8192]{1,0:T(8,128)S(1)} %collective-permute-done.12), channel_id=1, source_target_pairs={{0,8},{2,10},{8,16},{10,18},{16,24},{18,26},{24,28},{26,30},{28,20... | collective-permute-start | bytes 3145736 | tf_op jit(solution)/shard_map/ppermute | solution.py:55
  153.2 23.6 %collective-permute-start.16 = (f32[32,8192]{1,0:T(8,128)S(1)}, f32[32,8192]{1,0:T(8,128)}, u32[]{:S(2)}, u32[]{:S(2)}) collective-permute-start(f32[32,8192]{1,0:T(8,128)S(1)} %collective-permute-done.13), channel_id=1, source_target_pairs={{8,0},{10,2},{16,8},{18,10},{24,16},{26,18},{28,24},{30,26},{20,28... | collective-permute-start | bytes 3145736 | tf_op jit(solution)/shard_map/ppermute | solution.py:56
  155.0 14.8 %collective-permute-start.17 = (f32[64,8192]{1,0:T(8,128)}, f32[64,8192]{1,0:T(8,128)}, u32[]{:S(2)}, u32[]{:S(2)}) collective-permute-start(f32[64,8192]{1,0:T(8,128)} %pad_maximum_fusion.12), channel_id=1, source_target_pairs={{0,2},{2,0},{4,6},{6,4},{8,10},{10,8},{12,14},{14,12},{16,18},{18,... | collective-permute-start | bytes 6291464 | tf_op jit(solution)/shard_map/ppermute | solution.py:58
  176.9 22.7 %collective-permute-start.18 = (f32[32,8192]{1,0:T(8,128)S(1)}, f32[32,8192]{1,0:T(8,128)S(1)}, u32[]{:S(2)}, u32[]{:S(2)}) collective-permute-start(f32[32,8192]{1,0:T(8,128)S(1)} %collective-permute-done.15), channel_id=1, source_target_pairs={{0,8},{2,10},{8,16},{10,18},{16,24},{18,26},{24,28},{26,30},{28,20... | collective-permute-start | bytes 3145736 | tf_op jit(solution)/shard_map/ppermute | solution.py:55
  178.4 23.7 %collective-permute-start.19 = (f32[32,8192]{1,0:T(8,128)}, f32[32,8192]{1,0:T(8,128)S(1)}, u32[]{:S(2)}, u32[]{:S(2)}) collective-permute-start(f32[32,8192]{1,0:T(8,128)} %collective-permute-done.16), channel_id=1, source_target_pairs={{8,0},{10,2},{16,8},{18,10},{24,16},{26,18},{28,24},{30,26},{20,28... | collective-permute-start | bytes 3145736 | tf_op jit(solution)/shard_map/ppermute | solution.py:56
  181.8 15.3 %collective-permute-start.20 = (f32[64,8192]{1,0:T(8,128)}, f32[64,8192]{1,0:T(8,128)}, u32[]{:S(2)}, u32[]{:S(2)}) collective-permute-start(f32[64,8192]{1,0:T(8,128)} %pad_maximum_fusion.13), channel_id=1, source_target_pairs={{0,2},{2,0},{4,6},{6,4},{8,10},{10,8},{12,14},{14,12},{16,18},{18,... | collective-permute-start | bytes 6291464 | tf_op jit(solution)/shard_map/ppermute | solution.py:58
  191.7 4.5 copy-start.7
  199.5 2.6 copy-start.4
  207.9 18.4 %collective-permute-start.21 = (f32[64,8192]{1,0:T(8,128)}, f32[64,8192]{1,0:T(8,128)}, u32[]{:S(2)}, u32[]{:S(2)}) collective-permute-start(f32[64,8192]{1,0:T(8,128)} %pad_maximum_fusion.14), channel_id=1, source_target_pairs={{0,2},{2,0},{4,6},{6,4},{8,10},{10,8},{12,14},{14,12},{16,18},{18,... | collective-permute-start | bytes 6291464 | tf_op jit(solution)/shard_map/ppermute | solution.py:58
  264.8 8.3 %copy-start.9 = (s32[1024]{0:T(1024)S(1)}, s32[1024]{0:T(1024)}, u32[]{:S(2)}) copy-start(s32[1024]{0:T(1024)} %iota_add_fusion) | copy-start | bytes 12292
  264.8 8.3 %copy-start.10 = (s32[128]{0:T(128)S(1)}, s32[128]{0:T(128)}, u32[]{:S(2)}) copy-start(s32[128]{0:T(128)} %get-tuple-element.175) | copy-start | bytes 1540
  264.8 8.3 %copy-start.11 = (s32[128]{0:T(128)S(1)}, s32[128]{0:T(128)}, u32[]{:S(2)}) copy-start(s32[128]{0:T(128)} %get-tuple-element.176) | copy-start | bytes 1540
  264.8 8.3 %copy-start.12 = (s32[128]{0:T(128)S(1)}, s32[128]{0:T(128)}, u32[]{:S(2)}) copy-start(s32[128]{0:T(128)} %get-tuple-element.177) | copy-start | bytes 1540
  264.8 8.3 %copy-start.13 = (s32[128]{0:T(128)S(1)}, s32[128]{0:T(128)}, u32[]{:S(2)}) copy-start(s32[128]{0:T(128)} %get-tuple-element.178) | copy-start | bytes 1540
  275.1 14.4 %collective-permute-start.22 = (f32[128,1024]{1,0:T(8,128)S(1)}, f32[128,1024]{1,0:T(8,128)S(1)}, u32[]{:S(2)}, u32[]{:S(2)}) collective-permute-start(f32[128,1024]{1,0:T(8,128)S(1)} %get-tuple-element.158), channel_id=1, source_target_pairs={{0,1},{1,0},{2,3},{3,2},{4,5},{5,4},{6,7},{7,6},{8,9},{9,8},{10,11... | collective-permute-start | bytes 1572872 | tf_op jit(solution)/shard_map/ppermute | solution.py:104
  320.2 14.9 %collective-permute-start.23 = (f32[64,8192]{1,0:T(8,128)S(1)}, f32[64,8192]{1,0:T(8,128)S(1)}, u32[]{:S(2)}, u32[]{:S(2)}) collective-permute-start(f32[64,8192]{1,0:T(8,128)S(1)} %slice.243), channel_id=1, source_target_pairs={{0,2},{2,0},{4,6},{6,4},{8,10},{10,8},{12,14},{14,12},{16,18},{18,... | collective-permute-start | bytes 6291464 | tf_op jit(solution)/shard_map/ppermute | solution.py:121
  320.2 14.8 %collective-permute-start.24 = (f32[128,1024]{1,0:T(8,128)S(1)}, f32[128,1024]{1,0:T(8,128)S(1)}, u32[]{:S(2)}, u32[]{:S(2)}) collective-permute-start(f32[128,1024]{1,0:T(8,128)S(1)} %get-tuple-element.156), channel_id=1, source_target_pairs={{0,1},{1,0},{2,3},{3,2},{4,5},{5,4},{6,7},{7,6},{8,9},{9,8},{10,11... | collective-permute-start | bytes 1572872 | tf_op jit(solution)/shard_map/ppermute | solution.py:104
  321.8 47.6 %collective-permute-start.28 = (f32[128,1024]{1,0:T(8,128)S(1)}, f32[128,1024]{1,0:T(8,128)}, u32[]{:S(2)}, u32[]{:S(2)}) collective-permute-start(f32[128,1024]{1,0:T(8,128)S(1)} %get-tuple-element.157), channel_id=1, source_target_pairs={{0,1},{1,0},{2,3},{3,2},{4,5},{5,4},{6,7},{7,6},{8,9},{9,8},{10,11... | collective-permute-start | bytes 1572872 | tf_op jit(solution)/shard_map/ppermute | solution.py:104
  336.4 27.8 %collective-permute-start.25 = (f32[16,8192]{1,0:T(8,128)}, f32[16,8192]{1,0:T(8,128)}, u32[]{:S(2)}, u32[]{:S(2)}) collective-permute-start(f32[16,8192]{1,0:T(8,128)} %get-tuple-element.146), channel_id=1, source_target_pairs={{0,8},{2,10},{8,16},{10,18},{16,24},{18,26},{24,28},{26,30},{28,20... | collective-permute-start | bytes 1572872 | tf_op jit(solution)/shard_map/ppermute | solution.py:136
  337.3 26.9 %collective-permute-start.26 = (f32[16,8192]{1,0:T(8,128)}, f32[16,8192]{1,0:T(8,128)}, u32[]{:S(2)}, u32[]{:S(2)}) collective-permute-start(f32[16,8192]{1,0:T(8,128)} %get-tuple-element.145), channel_id=1, source_target_pairs={{8,0},{10,2},{16,8},{18,10},{24,16},{26,18},{28,24},{30,26},{20,28... | collective-permute-start | bytes 1572872 | tf_op jit(solution)/shard_map/ppermute | solution.py:137
  364.4 16.4 %collective-permute-start.27 = (f32[64,8192]{1,0:T(8,128)S(1)}, f32[64,8192]{1,0:T(8,128)S(1)}, u32[]{:S(2)}, u32[]{:S(2)}) collective-permute-start(f32[64,8192]{1,0:T(8,128)S(1)} %slice.169), channel_id=1, source_target_pairs={{0,2},{2,0},{4,6},{6,4},{8,10},{10,8},{12,14},{14,12},{16,18},{18,... | collective-permute-start | bytes 6291464 | tf_op jit(solution)/shard_map/ppermute | solution.py:121
  365.8 14.4 %collective-permute-start.29 = (f32[16,8192]{1,0:T(8,128)S(1)}, f32[16,8192]{1,0:T(8,128)S(1)}, u32[]{:S(2)}, u32[]{:S(2)}) collective-permute-start(f32[16,8192]{1,0:T(8,128)S(1)} %get-tuple-element.144), channel_id=1, source_target_pairs={{0,8},{2,10},{8,16},{10,18},{16,24},{18,26},{24,28},{26,30},{28,20... | collective-permute-start | bytes 1572872 | tf_op jit(solution)/shard_map/ppermute | solution.py:136
  366.8 14.0 %collective-permute-start.30 = (f32[16,8192]{1,0:T(8,128)S(1)}, f32[16,8192]{1,0:T(8,128)S(1)}, u32[]{:S(2)}, u32[]{:S(2)}) collective-permute-start(f32[16,8192]{1,0:T(8,128)S(1)} %get-tuple-element.143), channel_id=1, source_target_pairs={{8,0},{10,2},{16,8},{18,10},{24,16},{26,18},{28,24},{30,26},{20,28... | collective-permute-start | bytes 1572872 | tf_op jit(solution)/shard_map/ppermute | solution.py:137
  367.9 50.1 %collective-permute-start.34 = (f32[128,1024]{1,0:T(8,128)S(1)}, f32[128,1024]{1,0:T(8,128)}, u32[]{:S(2)}, u32[]{:S(2)}) collective-permute-start(f32[128,1024]{1,0:T(8,128)S(1)} %get-tuple-element.155), channel_id=1, source_target_pairs={{0,1},{1,0},{2,3},{3,2},{4,5},{5,4},{6,7},{7,6},{8,9},{9,8},{10,11... | collective-permute-start | bytes 1572872 | tf_op jit(solution)/shard_map/ppermute | solution.py:104
  382.2 32.1 %collective-permute-start.31 = (f32[16,8192]{1,0:T(8,128)}, f32[16,8192]{1,0:T(8,128)}, u32[]{:S(2)}, u32[]{:S(2)}) collective-permute-start(f32[16,8192]{1,0:T(8,128)} %get-tuple-element.142), channel_id=1, source_target_pairs={{0,8},{2,10},{8,16},{10,18},{16,24},{18,26},{24,28},{26,30},{28,20... | collective-permute-start | bytes 1572872 | tf_op jit(solution)/shard_map/ppermute | solution.py:136
  382.8 31.5 %collective-permute-start.32 = (f32[16,8192]{1,0:T(8,128)}, f32[16,8192]{1,0:T(8,128)}, u32[]{:S(2)}, u32[]{:S(2)}) collective-permute-start(f32[16,8192]{1,0:T(8,128)} %get-tuple-element.141), channel_id=1, source_target_pairs={{8,0},{10,2},{16,8},{18,10},{24,16},{26,18},{28,24},{30,26},{20,28... | collective-permute-start | bytes 1572872 | tf_op jit(solution)/shard_map/ppermute | solution.py:137
  414.4 16.2 %collective-permute-start.33 = (f32[64,8192]{1,0:T(8,128)S(1)}, f32[64,8192]{1,0:T(8,128)S(1)}, u32[]{:S(2)}, u32[]{:S(2)}) collective-permute-start(f32[64,8192]{1,0:T(8,128)S(1)} %slice.177), channel_id=1, source_target_pairs={{0,2},{2,0},{4,6},{6,4},{8,10},{10,8},{12,14},{14,12},{16,18},{18,... | collective-permute-start | bytes 6291464 | tf_op jit(solution)/shard_map/ppermute | solution.py:121
  415.9 14.4 %collective-permute-start.35 = (f32[16,8192]{1,0:T(8,128)S(1)}, f32[16,8192]{1,0:T(8,128)S(1)}, u32[]{:S(2)}, u32[]{:S(2)}) collective-permute-start(f32[16,8192]{1,0:T(8,128)S(1)} %get-tuple-element.140), channel_id=1, source_target_pairs={{0,8},{2,10},{8,16},{10,18},{16,24},{18,26},{24,28},{26,30},{28,20... | collective-permute-start | bytes 1572872 | tf_op jit(solution)/shard_map/ppermute | solution.py:136
  416.6 14.0 %collective-permute-start.36 = (f32[16,8192]{1,0:T(8,128)S(1)}, f32[16,8192]{1,0:T(8,128)S(1)}, u32[]{:S(2)}, u32[]{:S(2)}) collective-permute-start(f32[16,8192]{1,0:T(8,128)S(1)} %get-tuple-element.139), channel_id=1, source_target_pairs={{8,0},{10,2},{16,8},{18,10},{24,16},{26,18},{28,24},{30,26},{20,28... | collective-permute-start | bytes 1572872 | tf_op jit(solution)/shard_map/ppermute | solution.py:137
  432.0 32.3 %collective-permute-start.37 = (f32[16,8192]{1,0:T(8,128)}, f32[16,8192]{1,0:T(8,128)S(1)}, u32[]{:S(2)}, u32[]{:S(2)}) collective-permute-start(f32[16,8192]{1,0:T(8,128)} %get-tuple-element.138), channel_id=1, source_target_pairs={{0,8},{2,10},{8,16},{10,18},{16,24},{18,26},{24,28},{26,30},{28,20... | collective-permute-start | bytes 1572872 | tf_op jit(solution)/shard_map/ppermute | solution.py:136
  432.4 31.9 %collective-permute-start.38 = (f32[16,8192]{1,0:T(8,128)}, f32[16,8192]{1,0:T(8,128)}, u32[]{:S(2)}, u32[]{:S(2)}) collective-permute-start(f32[16,8192]{1,0:T(8,128)} %get-tuple-element.137), channel_id=1, source_target_pairs={{8,0},{10,2},{16,8},{18,10},{24,16},{26,18},{28,24},{30,26},{20,28... | collective-permute-start | bytes 1572872 | tf_op jit(solution)/shard_map/ppermute | solution.py:137
  464.4 15.8 %collective-permute-start.39 = (f32[64,8192]{1,0:T(8,128)S(1)}, f32[64,8192]{1,0:T(8,128)S(1)}, u32[]{:S(2)}, u32[]{:S(2)}) collective-permute-start(f32[64,8192]{1,0:T(8,128)S(1)} %slice.185), channel_id=1, source_target_pairs={{0,2},{2,0},{4,6},{6,4},{8,10},{10,8},{12,14},{14,12},{16,18},{18,... | collective-permute-start | bytes 6291464 | tf_op jit(solution)/shard_map/ppermute | solution.py:121
  465.7 14.4 %collective-permute-start.40 = (f32[16,8192]{1,0:T(8,128)S(1)}, f32[16,8192]{1,0:T(8,128)S(1)}, u32[]{:S(2)}, u32[]{:S(2)}) collective-permute-start(f32[16,8192]{1,0:T(8,128)S(1)} %get-tuple-element.136), channel_id=1, source_target_pairs={{0,8},{2,10},{8,16},{10,18},{16,24},{18,26},{24,28},{26,30},{28,20... | collective-permute-start | bytes 1572872 | tf_op jit(solution)/shard_map/ppermute | solution.py:136
  466.2 14.0 %collective-permute-start.41 = (f32[16,8192]{1,0:T(8,128)S(1)}, f32[16,8192]{1,0:T(8,128)S(1)}, u32[]{:S(2)}, u32[]{:S(2)}) collective-permute-start(f32[16,8192]{1,0:T(8,128)S(1)} %get-tuple-element.135), channel_id=1, source_target_pairs={{8,0},{10,2},{16,8},{18,10},{24,16},{26,18},{28,24},{30,26},{20,28... | collective-permute-start | bytes 1572872 | tf_op jit(solution)/shard_map/ppermute | solution.py:137
  480.3 15.1 %copy-start.1 = (s32[512]{0:T(512)S(1)}, s32[512]{0:T(512)}, u32[]{:S(2)}) copy-start(s32[512]{0:T(512)} %param.7) | copy-start | bytes 6148
  480.6 13.4 %collective-permute-start.42 = (f32[16,8192]{1,0:T(8,128)S(1)}, f32[16,8192]{1,0:T(8,128)S(1)}, u32[]{:S(2)}, u32[]{:S(2)}) collective-permute-start(f32[16,8192]{1,0:T(8,128)S(1)} %get-tuple-element.134), channel_id=1, source_target_pairs={{0,8},{2,10},{8,16},{10,18},{16,24},{18,26},{24,28},{26,30},{28,20... | collective-permute-start | bytes 1572872 | tf_op jit(solution)/shard_map/ppermute | solution.py:136
  481.2 13.0 %collective-permute-start.43 = (f32[16,8192]{1,0:T(8,128)S(1)}, f32[16,8192]{1,0:T(8,128)S(1)}, u32[]{:S(2)}, u32[]{:S(2)}) collective-permute-start(f32[16,8192]{1,0:T(8,128)S(1)} %get-tuple-element.133), channel_id=1, source_target_pairs={{8,0},{10,2},{16,8},{18,10},{24,16},{26,18},{28,24},{30,26},{20,28... | collective-permute-start | bytes 1572872 | tf_op jit(solution)/shard_map/ppermute | solution.py:137
